TPU v7x, 32 devices: a whole 2x2x4 slice. The times are simulated.
32 devices in a mesh: grp: 2 (over x), seq: 8 (over z, y), head: 2 (over core).
Axes of the slice: x: 2, y: 2, z: 4, core: 2. Of those that a mesh axis runs over, the one named last changes fastest.
Arguments:
- prompt_hidden: bfloat16 [16, 128, 5120], P(('grp', 'seq')), parts along dimension 0, may hold values from -6 to 6
- key_weight: bfloat16 [5120, 512], P('seq', 'head'), may hold values from -0.078125 to 0.078125
- value_weight: bfloat16 [5120, 512], P('seq', 'head'), may hold values from -0.078125 to 0.078125
- queries: bfloat16 [32, 512, 2560], P(('grp', 'seq'), None, 'head'), parts along dimension 0
- resp_keys: bfloat16 [32, 512, 512], P(('grp', 'seq'), None, 'head'), parts along dimension 0
- resp_values: bfloat16 [32, 512, 512], P(('grp', 'seq'), None, 'head'), parts along dimension 0, may hold values from -6 to 6
- out_grad: bfloat16 [32, 512, 2560], P(('grp', 'seq'), None, 'head'), parts along dimension 0, may hold values from -6 to 6
- counts: int32 [16], P('grp'), parts along dimension 0, may hold values from 1 to 8, 16 in all
- slot_of: int32 [32], P('grp'), parts along dimension 0, may hold values from 0 to 15, each once
- owner: int32 [16], P('grp'), parts along dimension 0, may hold values from 0 to 7, each once
Outputs:
- query_grad: bfloat16 [32, 512, 2560], P(('grp', 'seq'), None, 'head'), parts along dimension 0
- resp_key_grad: bfloat16 [32, 512, 512], P(('grp', 'seq'), None, 'head'), parts along dimension 0
- resp_value_grad: bfloat16 [32, 512, 512], P(('grp', 'seq'), None, 'head'), parts along dimension 0
- prompt_grad: bfloat16 [16, 128, 5120], P(('grp', 'seq'), None, 'head'), parts along dimension 0
There are 2 independent parts, one for each index of `grp`. A program takes and returns all parts, laid end to end along the dimension named above; an argument that names none is the same for every part. Nothing has to cross between parts.
Inputs may be any that keep to these rules, and one draw needn't show every extreme that they name: `counts`: every prompt has one response or more; they add up to 16, and the largest is exactly 8. `slot_of`: A permutation: responses are numbered prompt by prompt in the order of counts; slot s is row s of the slot arrays. `owner`: A permutation.
All inputs are finite; a program needn't handle non-finite values.
Results may differ from a plain program's by a relative error of at most 0.012.
Values may be sent and summed in bfloat16 or wider, within the bound.
A program may use at most 128 MiB of HBM per device.

v0:
```python
import math

import jax
import jax.numpy as jnp
from jax import lax
from jax.sharding import PartitionSpec as P

HD = 128


def locate(counts, slot_of, owner, first, number):
    wanted = first + jnp.arange(number, dtype=jnp.int32)
    numbers = jnp.arange(slot_of.shape[0], dtype=jnp.int32)
    response = jnp.sum(jnp.where(slot_of[None, :] == wanted[:, None], numbers[None, :], 0), axis=1)
    ends = jnp.cumsum(counts)
    prompt = jnp.sum((ends[None, :] <= response[:, None]).astype(jnp.int32), axis=1)
    blocks = jnp.arange(owner.shape[0], dtype=jnp.int32)
    return jnp.sum(jnp.where(blocks[None, :] == prompt[:, None], owner[None, :], 0), axis=1)


def attend(query, key, value, grad, plen):
    rows = query.shape[0]
    keys = key.shape[0]
    heads_kv = key.shape[1] // HD
    group = query.shape[1] // (heads_kv * HD)
    scale = 1.0 / math.sqrt(HD)
    query_heads = query.reshape(rows, heads_kv, group, HD)
    grad_heads = grad.reshape(rows, heads_kv, group, HD)
    key_heads = key.reshape(keys, heads_kv, HD)
    value_heads = value.reshape(keys, heads_kv, HD)
    scores = (
        jnp.einsum("tkgd,ukd->kgtu", query_heads, key_heads, preferred_element_type=jnp.float32)
        * scale
    )
    visible = jnp.arange(keys)[None, :] - plen <= jnp.arange(rows)[:, None]
    scores = jnp.where(visible, scores, -jnp.inf)
    highest = jnp.max(scores, axis=-1, keepdims=True)
    weights = jnp.exp(scores - highest)
    probs = weights / jnp.sum(weights, axis=-1, keepdims=True)
    probs_b = probs.astype(jnp.bfloat16)
    attended = jnp.einsum(
        "kgtu,ukd->tkgd", probs_b, value_heads, preferred_element_type=jnp.float32
    ).astype(jnp.bfloat16)
    delta = jnp.transpose(
        jnp.sum(grad_heads.astype(jnp.float32) * attended.astype(jnp.float32), axis=-1), (1, 2, 0)
    )
    dprob = jnp.einsum(
        "tkgd,ukd->kgtu", grad_heads, value_heads, preferred_element_type=jnp.float32
    )
    dscore = (probs * (dprob - delta[..., None])).astype(jnp.bfloat16)
    grad_query = (
        jnp.einsum("kgtu,ukd->tkgd", dscore, key_heads, preferred_element_type=jnp.float32) * scale
    ).astype(jnp.bfloat16)
    grad_key = (
        jnp.einsum("kgtu,tkgd->ukd", dscore, query_heads, preferred_element_type=jnp.float32)
        * scale
    )
    grad_value = jnp.einsum(
        "kgtu,tkgd->ukd", probs_b, grad_heads, preferred_element_type=jnp.float32
    )
    return (grad_query.reshape(rows, -1), grad_key.reshape(keys, -1), grad_value.reshape(keys, -1))


def shards(
    prompt_hidden,
    key_weight,
    value_weight,
    queries,
    resp_keys,
    resp_values,
    out_grad,
    counts,
    slot_of,
    owner,
):
    slots = queries.shape[0]
    plen = prompt_hidden.shape[1]
    prompts = counts.shape[0]
    key_full, value_full = (
        lax.all_gather(key_weight, "seq", axis=0, tiled=True),
        lax.all_gather(value_weight, "seq", axis=0, tiled=True),
    )
    hidden = prompt_hidden[0]
    prompt_keys = jnp.dot(hidden, key_full, preferred_element_type=jnp.float32).astype(jnp.bfloat16)
    prompt_values = jnp.dot(hidden, value_full, preferred_element_type=jnp.float32).astype(
        jnp.bfloat16
    )
    first = lax.axis_index("seq") * slots
    blocks = locate(counts, slot_of, owner, first, slots)
    every_keys, every_values = (
        lax.all_gather(prompt_keys[None], "seq", axis=0, tiled=True),
        lax.all_gather(prompt_values[None], "seq", axis=0, tiled=True),
    )
    slot_keys = every_keys[blocks]
    slot_values = every_values[blocks]

    def one_slot(items):
        query, own_key, own_value, grad, taken_key, taken_value = items
        key = jnp.concatenate([taken_key, own_key], axis=0)
        value = jnp.concatenate([taken_value, own_value], axis=0)
        return attend(query, key, value, grad, plen)

    grad_query, grad_key, grad_value = lax.map(
        one_slot, (queries, resp_keys, resp_values, out_grad, slot_keys, slot_values)
    )
    prompt_part_key = grad_key[:, :plen]
    prompt_part_value = grad_value[:, :plen]
    hits = (blocks[:, None] == jnp.arange(prompts, dtype=jnp.int32)[None, :]).astype(jnp.float32)
    term_key = jnp.einsum("rp,rlc->plc", hits, prompt_part_key, precision=lax.Precision.HIGHEST)
    term_value = jnp.einsum("rp,rlc->plc", hits, prompt_part_value, precision=lax.Precision.HIGHEST)
    back_key, back_value = (
        lax.psum_scatter(term_key, "seq", scatter_dimension=0, tiled=True),
        lax.psum_scatter(term_value, "seq", scatter_dimension=0, tiled=True),
    )
    key_rows = back_key[0].astype(jnp.bfloat16)
    value_rows = back_value[0].astype(jnp.bfloat16)
    partial_grad = jnp.einsum("lc,dc->ld", key_rows, key_full, preferred_element_type=jnp.float32)
    partial_grad = partial_grad + jnp.einsum(
        "lc,dc->ld", value_rows, value_full, preferred_element_type=jnp.float32
    )
    prompt_grad = lax.psum_scatter(
        partial_grad[None].astype(jnp.bfloat16), "head", scatter_dimension=2, tiled=True
    )
    return (
        grad_query,
        grad_key[:, plen:].astype(jnp.bfloat16),
        grad_value[:, plen:].astype(jnp.bfloat16),
        prompt_grad,
    )


def solution(mesh):
    placed = (
        P(("grp", "seq"), None, None),
        P("seq", "head"),
        P("seq", "head"),
        P(("grp", "seq"), None, "head"),
        P(("grp", "seq"), None, "head"),
        P(("grp", "seq"), None, "head"),
        P(("grp", "seq"), None, "head"),
        P("grp"),
        P("grp"),
        P("grp"),
    )
    return jax.shard_map(
        shards,
        mesh=mesh,
        in_specs=placed,
        out_specs=(
            P(("grp", "seq"), None, "head"),
            P(("grp", "seq"), None, "head"),
            P(("grp", "seq"), None, "head"),
            P(("grp", "seq"), None, "head"),
        ),
        check_vma=False,
    )
```

profile of v0, /device:TPU:0, one launch (start us, length us, event | category | flops | bytes accessed | tf_op | source)
XLA Modules:
  0.0 419.8 jit_solution(3528199863087326840)
XLA Ops:
  12.0 55.5 %all-gather.5.cloned.1.call-done = bf16[5120,256]{1,0:T(8,128)(2,1)} async-done(((bf16[640,256]{1,0:T(8,128)(2,1)}), bf16[5120,256]{1,0:T(8,128)(2,1)}) %all-gather.5.cloned.1.call-update) | async-done | bytes 2621456 | tf_op jit(solution)/shard_map/all_gather | solution.py:80
  67.6 2.2 fusion.28
  69.8 32.8 %all-gather = bf16[1024,256]{1,0:T(8,128)(2,1)S(1)} all-gather(bf16[128,256]{1,0:T(8,128)(2,1)S(1)} %fusion.28), channel_id=2, replica_groups=mesh['grp'=2,'seq'=8,'head'=2] {'seq'}, dimensions={0}, use_global_device_ids=true | all-gather | bytes 589824 | tf_op jit(solution)/shard_map/all_gather | solution.py:91
  102.7 22.6 %all-gather.7.cloned.1.call-done = bf16[5120,256]{1,0:T(8,128)(2,1)} async-done(((bf16[640,256]{1,0:T(8,128)(2,1)}), bf16[5120,256]{1,0:T(8,128)(2,1)}) %all-gather.7.cloned.1.call-update) | async-done | bytes 2621456 | tf_op jit(solution)/shard_map/all_gather | solution.py:81
  125.3 2.2 fusion.31
  127.5 31.7 %all-gather.1 = bf16[1024,256]{1,0:T(8,128)(2,1)S(1)} all-gather(bf16[128,256]{1,0:T(8,128)(2,1)S(1)} %fusion.31), channel_id=3, replica_groups=mesh['grp'=2,'seq'=8,'head'=2] {'seq'}, dimensions={0}, use_global_device_ids=true | all-gather | bytes 589824 | tf_op jit(solution)/shard_map/all_gather | solution.py:92
  161.6 104.6 %while.16 = (s32[]{:T(128)}, bf16[2,512,1280]{2,1,0:T(8,128)(2,1)}, f32[2,640,256]{1,2,0:T(8,128)}, f32[2,640,256]{1,2,0:T(8,128)}, bf16[2,128,256]{2,1,0:T(8,12...) while((s32[]{:T(128)}, bf16[2,512,1280]{2,1,0:T(8,128)(2,1)}, ...), condition=%wide.region_8.9_spmd, body=%wide.region_4.8_spmd.sunk | while | flops 5073629184 | bytes 159622608 | solution.py:103
  167.4 1.4 constant_dynamic-slice_fusion.12
  170.9 1.5 copy.158
  172.4 10.5 %fusion.88 = (f32[2,5,512]{2,1,0:T(8,128)S(1)}, f32[2,5,512,640]{2,3,1,0:T(8,128)}) fusion(pred[512,640]{0,1:T(8,128)(4,1)S(1)} %iota_compare_fusion.5, bf16[512,2,5,128]{0,3,2,1:T(8,128)(2,1)} %bitcast.171, bf16[512,2,128]{2,0,1:T(8,128)(2,1)S(1)} %copy.160, bf16[128,2,128]{2,0,1:T(8,128)(2,1)S(1)} %copy.162), kind=kOutput, calls=%fused_computation.77.clone.1 | convolution fusion | flops 852624000 | bytes 15093760 | tf_op jit(solution)/shard_map/while/body/eval_jaxpr/sub | solution.py:38
  182.9 9.4 %fusion.89 = bf16[2,5,512,640]{2,3,1,0:T(8,128)(2,1)} fusion(f32[2,5,512,640]{2,3,1,0:T(8,128)} %get-tuple-element.283, f32[2,5,512]{2,1,0:T(8,128)S(1)} %get-tuple-element.284), kind=kLoop, calls=%fused_computation.13.clone.1 | loop fusion | flops 6553600 | bytes 19681280 | tf_op jit(solution)/shard_map/while/body/eval_jaxpr/convert_element_type | solution.py:40
  192.3 4.3 %fusion.90 = f32[512,2,5]{0,2,1:T(8,128)S(1)} fusion(bf16[512,2,5,128]{0,3,2,1:T(8,128)(2,1)S(1)} %bitcast.167, bf16[2,5,512,640]{2,3,1,0:T(8,128)(2,1)} %fusion.89, bf16[512,2,128]{2,0,1:T(8,128)(2,1)S(1)} %copy.164, bf16[128,2,128]{2,0,1:T(8,128)(2,1)S(1)} %copy-done.9), kind=kOutput, calls=%fused_computation.15.clone.1 | convolution fusion | flops 842787840 | bytes 8212480 | tf_op jit(solution)/shard_map/while/body/eval_jaxpr/kgtu,ukd->tkgd/dot_general | solution.py:41
  197.0 2.1 fusion.92
  199.1 5.9 %fusion.91 = bf16[2,5,512,640]{2,3,1,0:T(8,128)(2,1)S(1)} fusion(f32[2,5,512]{2,1,0:T(8,128)S(1)} %bitcast.179, bf16[512,2,5,128]{0,3,2,1:T(8,128)(2,1)S(1)} %bitcast.169, f32[2,5,512,640]{2,3,1,0:T(8,128)} %get-tuple-element.283, f32[2,5,512]{2,1,0:T(8,128)S(1)} %get-tuple-element.284, bf16[512,2,128]{2,0,1:T(8,128)(2,1)S(1)} %copy-done.6, ...), kind=kOutput, calls=%fused_computation.5.clone.1 | convolution fusion | flops 852623360 | bytes 21340160 | tf_op jit(solution)/shard_map/while/body/eval_jaxpr/tkgd,ukd->kgtu/dot_general | solution.py:47
  205.1 2.9 fusion.93
  223.2 1.5 copy.158
  224.7 10.5 %fusion.88 = (f32[2,5,512]{2,1,0:T(8,128)S(1)}, f32[2,5,512,640]{2,3,1,0:T(8,128)}) fusion(pred[512,640]{0,1:T(8,128)(4,1)S(1)} %iota_compare_fusion.5, bf16[512,2,5,128]{0,3,2,1:T(8,128)(2,1)} %bitcast.171, bf16[512,2,128]{2,0,1:T(8,128)(2,1)S(1)} %copy.160, bf16[128,2,128]{2,0,1:T(8,128)(2,1)S(1)} %copy.162), kind=kOutput, calls=%fused_computation.77.clone.1 | convolution fusion | flops 852624000 | bytes 15093760 | tf_op jit(solution)/shard_map/while/body/eval_jaxpr/sub | solution.py:38
  235.2 9.4 %fusion.89 = bf16[2,5,512,640]{2,3,1,0:T(8,128)(2,1)} fusion(f32[2,5,512,640]{2,3,1,0:T(8,128)} %get-tuple-element.283, f32[2,5,512]{2,1,0:T(8,128)S(1)} %get-tuple-element.284), kind=kLoop, calls=%fused_computation.13.clone.1 | loop fusion | flops 6553600 | bytes 19681280 | tf_op jit(solution)/shard_map/while/body/eval_jaxpr/convert_element_type | solution.py:40
  244.6 4.3 %fusion.90 = f32[512,2,5]{0,2,1:T(8,128)S(1)} fusion(bf16[512,2,5,128]{0,3,2,1:T(8,128)(2,1)S(1)} %bitcast.167, bf16[2,5,512,640]{2,3,1,0:T(8,128)(2,1)} %fusion.89, bf16[512,2,128]{2,0,1:T(8,128)(2,1)S(1)} %copy.164, bf16[128,2,128]{2,0,1:T(8,128)(2,1)S(1)} %copy-done.9), kind=kOutput, calls=%fused_computation.15.clone.1 | convolution fusion | flops 842787840 | bytes 8212480 | tf_op jit(solution)/shard_map/while/body/eval_jaxpr/kgtu,ukd->tkgd/dot_general | solution.py:41
  249.3 2.1 fusion.92
  251.4 5.9 %fusion.91 = bf16[2,5,512,640]{2,3,1,0:T(8,128)(2,1)S(1)} fusion(f32[2,5,512]{2,1,0:T(8,128)S(1)} %bitcast.179, bf16[512,2,5,128]{0,3,2,1:T(8,128)(2,1)S(1)} %bitcast.169, f32[2,5,512,640]{2,3,1,0:T(8,128)} %get-tuple-element.283, f32[2,5,512]{2,1,0:T(8,128)S(1)} %get-tuple-element.284, bf16[512,2,128]{2,0,1:T(8,128)(2,1)S(1)} %copy-done.6, ...), kind=kOutput, calls=%fused_computation.5.clone.1 | convolution fusion | flops 852623360 | bytes 21340160 | tf_op jit(solution)/shard_map/while/body/eval_jaxpr/tkgd,ukd->kgtu/dot_general | solution.py:47
  257.4 2.9 fusion.93
  266.3 3.3 copy.117
  269.6 1.8 fusion.36
  272.8 2.0 copy.119
  274.8 1.7 fusion.34
  277.9 56.5 %reduce-scatter.4.cloned.1.call-done = f32[1,128,256]{2,1,0:T(8,128)} async-done(((f32[8,128,256]{2,1,0:T(8,128)}), f32[1,128,256]{2,1,0:T(8,128)}) %reduce-scatter.4.cloned.1.call-update) | async-done | bytes 131088 | tf_op jit(solution)/shard_map/reduce_scatter | solution.py:112
  334.4 4.3 %fusion.39 = f32[128,5120]{1,0:T(8,128)} fusion(bf16[5120,256]{1,0:T(8,128)(2,1)} %all-gather.5.cloned.1.call-done, f32[1,128,256]{2,1,0:T(8,128)} %reduce-scatter.4.cloned.1.call-done), kind=kOutput, calls=%fused_computation.58 | convolution fusion | flops 335577088 | bytes 5373952 | tf_op jit(solution)/shard_map/lc,dc->ld/dot_general | solution.py:117
  338.7 61.8 %reduce-scatter.6.cloned.1.call-done = f32[1,128,256]{2,1,0:T(8,128)} async-done(((f32[8,128,256]{2,1,0:T(8,128)}), f32[1,128,256]{2,1,0:T(8,128)}) %reduce-scatter.6.cloned.1.call-update) | async-done | bytes 131088 | tf_op jit(solution)/shard_map/reduce_scatter | solution.py:113
  400.6 4.7 %fusion.23 = bf16[1,128,5120]{2,1,0:T(8,128)(2,1)} fusion(f32[128,5120]{1,0:T(8,128)} %fusion.39, bf16[5120,256]{1,0:T(8,128)(2,1)} %all-gather.7.cloned.1.call-done, f32[1,128,256]{2,1,0:T(8,128)} %reduce-scatter.6.cloned.1.call-done), kind=kOutput, calls=%fused_computation.44 | convolution fusion | flops 336887808 | bytes 6684672 | tf_op jit(solution)/shard_map/lc,dc->ld/dot_general | solution.py:118
  405.5 1.7 copy.115
  408.8 4.4 %reduce-scatter.8.cloned.1.call-done = bf16[1,128,2560]{2,1,0:T(8,128)(2,1)} async-done(((bf16[1,128,5120]{2,1,0:T(8,128)(2,1)}), bf16[1,128,2560]{2,1,0:T(8,128)(2,1)}) %reduce-scatter.8.cloned.1.call-update) | async-done | bytes 655376 | tf_op jit(solution)/shard_map/reduce_scatter | solution.py:121
  (118 shorter events, 41.6 us)
Async XLA Ops:
  7.2 60.4 %copy-start = (bf16[1,128,5120]{2,1,0:T(8,128)(2,1)S(1)}, bf16[1,128,5120]{2,1,0:T(8,128)(2,1)}, u32[]{:S(2)}) copy-start(bf16[1,128,5120]{2,1,0:T(8,128)(2,1)} %param.12) | copy-start | bytes 3932164
  7.2 60.4 %all-gather.5.cloned.1.call-start = ((), (), s32[]{:S(2)}) async-start(), calls=%async_computation.3 | async-start | bytes 2949120 | tf_op jit(solution)/shard_map/all_gather | solution.py:80
  7.9 117.4 %all-gather.7.cloned.1.call-start = ((), (), s32[]{:S(2)}) async-start(), calls=%async_computation.4 | async-start | bytes 2949120 | tf_op jit(solution)/shard_map/all_gather | solution.py:81
  8.7 325.8 %reduce-scatter.4.cloned.1.call-start = ((), (), s32[]{:S(2)}) async-start(), calls=%async_computation.5 | async-start | bytes 1179648 | tf_op jit(solution)/shard_map/reduce_scatter | solution.py:112
  11.4 0.6 copy-start.13
  164.4 8.0 %copy-start.7 = (bf16[128,2,128]{2,0,1:T(8,128)(2,1)}, bf16[128,2,128]{2,0,1:T(8,128)(2,1)S(1)}, u32[]{:S(2)}) copy-start(bf16[128,2,128]{2,0,1:T(8,128)(2,1)S(1)} %copy.162) | copy-start | bytes 196612 | tf_op jit(solution)/shard_map/while
  165.8 26.5 %copy-start.5 = (bf16[512,2,128]{2,0,1:T(8,128)(2,1)}, bf16[512,2,128]{2,0,1:T(8,128)(2,1)S(1)}, u32[]{:S(2)}) copy-start(bf16[512,2,128]{2,0,1:T(8,128)(2,1)S(1)} %copy.164) | copy-start | bytes 786436 | tf_op jit(solution)/shard_map/while
  182.9 9.4 %copy-start.9 = (bf16[128,2,128]{2,0,1:T(8,128)(2,1)S(1)}, bf16[128,2,128]{2,0,1:T(8,128)(2,1)}, u32[]{:S(2)}) copy-start(bf16[128,2,128]{2,0,1:T(8,128)(2,1)} %copy.166) | copy-start | bytes 196612 | tf_op jit(solution)/shard_map/while
  192.3 4.7 %copy-start.2 = (bf16[2,5,512,640]{2,3,1,0:T(8,128)(2,1)S(1)}, bf16[2,5,512,640]{2,3,1,0:T(8,128)(2,1)}, u32[]{:S(2)}) copy-start(bf16[2,5,512,640]{2,3,1,0:T(8,128)(2,1)} %fusion.89) | copy-start | bytes 19660804 | tf_op jit(solution)/shard_map/while
  197.0 2.1 copy-start.6
  199.1 5.9 %copy-start.3 = (bf16[1,512,1280]{1,2,0:T(8,128)(2,1)S(1)}, bf16[1,512,1280]{1,2,0:T(8,128)(2,1)}, u32[]{:S(2)}) copy-start(bf16[1,512,1280]{1,2,0:T(8,128)(2,1)} %copy.158) | copy-start | bytes 3932164 | tf_op jit(solution)/shard_map/while
  205.1 2.9 copy-start.8
  209.9 1.3 copy-start.4
  209.9 2.0 copy-start.10
  212.9 1.1 copy-start.11
  216.7 8.0 %copy-start.7 = (bf16[128,2,128]{2,0,1:T(8,128)(2,1)}, bf16[128,2,128]{2,0,1:T(8,128)(2,1)S(1)}, u32[]{:S(2)}) copy-start(bf16[128,2,128]{2,0,1:T(8,128)(2,1)S(1)} %copy.162) | copy-start | bytes 196612 | tf_op jit(solution)/shard_map/while
  218.1 26.5 %copy-start.5 = (bf16[512,2,128]{2,0,1:T(8,128)(2,1)}, bf16[512,2,128]{2,0,1:T(8,128)(2,1)S(1)}, u32[]{:S(2)}) copy-start(bf16[512,2,128]{2,0,1:T(8,128)(2,1)S(1)} %copy.164) | copy-start | bytes 786436 | tf_op jit(solution)/shard_map/while
  235.2 9.4 %copy-start.9 = (bf16[128,2,128]{2,0,1:T(8,128)(2,1)S(1)}, bf16[128,2,128]{2,0,1:T(8,128)(2,1)}, u32[]{:S(2)}) copy-start(bf16[128,2,128]{2,0,1:T(8,128)(2,1)} %copy.166) | copy-start | bytes 196612 | tf_op jit(solution)/shard_map/while
  244.6 4.7 %copy-start.2 = (bf16[2,5,512,640]{2,3,1,0:T(8,128)(2,1)S(1)}, bf16[2,5,512,640]{2,3,1,0:T(8,128)(2,1)}, u32[]{:S(2)}) copy-start(bf16[2,5,512,640]{2,3,1,0:T(8,128)(2,1)} %fusion.89) | copy-start | bytes 19660804 | tf_op jit(solution)/shard_map/while
  249.3 2.1 copy-start.6
  251.4 5.9 %copy-start.3 = (bf16[1,512,1280]{1,2,0:T(8,128)(2,1)S(1)}, bf16[1,512,1280]{1,2,0:T(8,128)(2,1)}, u32[]{:S(2)}) copy-start(bf16[1,512,1280]{1,2,0:T(8,128)(2,1)} %copy.158) | copy-start | bytes 3932164 | tf_op jit(solution)/shard_map/while
  257.4 2.9 copy-start.8
  262.2 1.3 copy-start.4
  262.2 2.0 copy-start.10
  265.2 1.1 copy-start.11
  266.3 3.3 copy-start.14
  269.6 3.2 copy-start.12
  272.7 127.9 %reduce-scatter.6.cloned.1.call-start = ((), (), s32[]{:S(2)}) async-start(), calls=%async_computation.6 | async-start | bytes 1179648 | tf_op jit(solution)/shard_map/reduce_scatter | solution.py:113
  277.9 135.4 %reduce-scatter.8.cloned.1.call-start = ((), (), s32[]{:S(2)}) async-start(), calls=%async_computation.7 | async-start | bytes 1966080 | tf_op jit(solution)/shard_map/reduce_scatter | solution.py:121
  405.3 8.0 %copy-start.1 = (bf16[1,128,5120]{2,1,0:T(8,128)(2,1)S(1)}, bf16[1,128,5120]{2,1,0:T(8,128)(2,1)}, u32[]{:S(2)}) copy-start(bf16[1,128,5120]{2,1,0:T(8,128)(2,1)} %param.12) | copy-start | bytes 3932164
Sparse Core Ops, SparseCore 0:
  10.2 57.3 all-gather.4
  69.8 55.4 all-gather.6
  272.8 61.5 reduce-scatter.3
  338.1 62.4 reduce-scatter.5
  405.4 7.8 reduce-scatter.7
where the time goes:
time: 421 us; the launch traced here: 420 us
  waiting for transfers between devices  202 us (48%)
  matrix products  70.9 us (17%)
  blocking collectives  64.5 us (15%)
  local copies, waits for them, and re-layouts  45.6 us (11%)
  other arithmetic  21.9 us (5%)
  between operations  13.9 us (3%)
    reduce_scatter x1, waiting for transfers between devices, shards(): lax.psum_scatter(term_value, 'seq', scatter_dimension=0, tiled=True)  61.8 us
    reduce_scatter x1, waiting for transfers between devices, shards(): lax.psum_scatter(term_key, 'seq', scatter_dimension=0, tiled=True)  56.5 us
    all_gather x1, waiting for transfers between devices, shards(): lax.all_gather(key_weight, 'seq', axis=0, tiled=True)  55.5 us
    all_gather x1, blocking collectives, shards(): lax.all_gather(prompt_keys[None], 'seq', axis=0, tiled=True)  32.8 us
    all_gather x1, blocking collectives, shards(): lax.all_gather(prompt_values[None], 'seq', axis=0, tiled=True)  31.7 us
    all_gather x1, waiting for transfers between devices, shards(): lax.all_gather(value_weight, 'seq', axis=0, tiled=True)  22.6 us
    sub x2, matrix products, attend(): weights = jnp.exp(scores - highest)  21.1 us
    convert_element_type x2, other arithmetic, attend(): probs_b = probs.astype(jnp.bfloat16)  18.7 us
  transfers between devices with their start and end apart: 5, of which 5 were waited for; matrix products, arithmetic and copies ran while one was open for 4% of the time, Pallas kernels for 0%

commit v1 on v0

v1 whole, which is shorter than its diff:
```python
import functools
import math

import jax
import jax.numpy as jnp
from jax import lax
from jax.experimental import pallas as pl
from jax.experimental.pallas import tpu as pltpu
from jax.sharding import PartitionSpec as P

HD = 128
CHUNK = 256


def locate(counts, slot_of, owner, first, number):
    wanted = first + jnp.arange(number, dtype=jnp.int32)
    numbers = jnp.arange(slot_of.shape[0], dtype=jnp.int32)
    response = jnp.sum(jnp.where(slot_of[None, :] == wanted[:, None], numbers[None, :], 0), axis=1)
    ends = jnp.cumsum(counts)
    prompt = jnp.sum((ends[None, :] <= response[:, None]).astype(jnp.int32), axis=1)
    blocks = jnp.arange(owner.shape[0], dtype=jnp.int32)
    return jnp.sum(jnp.where(blocks[None, :] == prompt[:, None], owner[None, :], 0), axis=1)


def dot(a, b, dims):
    return lax.dot_general(a, b, (dims, ((), ())), preferred_element_type=jnp.float32)


NT = ((1,), (1,))
NN = ((1,), (0,))


def attention_kernel(
    blocks_ref,
    query_ref,
    grad_ref,
    key_ref,
    value_ref,
    prompt_key_ref,
    prompt_value_ref,
    query_grad_ref,
    key_grad_ref,
    value_grad_ref,
    prompt_grad_key_ref,
    prompt_grad_value_ref,
    keys,
    keys_t,
    values,
    acc_key,
    acc_value,
):
    plen = prompt_key_ref.shape[1]
    rows = query_ref.shape[1]
    group = query_ref.shape[2] // HD
    scale = 1.0 / math.sqrt(HD)
    fold = scale * math.log2(math.e)
    keys[:plen, :] = prompt_key_ref[0]
    keys[plen:, :] = key_ref[0]
    values[:plen, :] = prompt_value_ref[0]
    values[plen:, :] = value_ref[0]
    keys_t[...] = keys[...].T
    acc_key[...] = jnp.zeros_like(acc_key)
    acc_value[...] = jnp.zeros_like(acc_value)
    later = lax.broadcasted_iota(jnp.int32, (CHUNK, CHUNK), 0) > lax.broadcasted_iota(
        jnp.int32, (CHUNK, CHUNK), 1
    )
    for part in range(rows // CHUNK):
        low = part * CHUNK
        edge = plen + low
        seen = edge + CHUNK
        for head in range(group):
            lanes = slice(head * HD, (head + 1) * HD)
            query = query_ref[0, low : low + CHUNK, lanes]
            grad = grad_ref[0, low : low + CHUNK, lanes]
            scores = dot(keys[:seen, :], query, NT)
            scores = jnp.concatenate(
                [scores[:edge], jnp.where(later, -jnp.inf, scores[edge:])], axis=0
            )
            highest = jnp.max(scores, axis=0, keepdims=True)
            weights = jnp.exp2((scores - highest) * fold)
            inverse = 1.0 / jnp.sum(weights, axis=0, keepdims=True)
            dprob = dot(values[:seen, :], grad, NT)
            probs = weights * inverse
            delta = jnp.sum(probs * dprob, axis=0, keepdims=True)
            dscore = (probs * (dprob - delta)).astype(jnp.bfloat16)
            acc_value[:seen, :] += dot(probs.astype(jnp.bfloat16), grad, NN)
            acc_key[:seen, :] += dot(dscore, query, NN)
            turned = dot(keys_t[:, :seen], dscore, NN) * scale
            query_grad_ref[0, low : low + CHUNK, lanes] = turned.T.astype(jnp.bfloat16)
    prompt_grad_key_ref[0] = (acc_key[:plen, :] * scale).astype(prompt_grad_key_ref.dtype)
    key_grad_ref[0] = (acc_key[plen:, :] * scale).astype(jnp.bfloat16)
    prompt_grad_value_ref[0] = acc_value[:plen, :].astype(prompt_grad_value_ref.dtype)
    value_grad_ref[0] = acc_value[plen:, :].astype(jnp.bfloat16)


def attention(blocks, queries, out_grad, resp_keys, resp_values, every):
    slots, rows, wide = queries.shape
    heads = resp_keys.shape[2] // HD
    group = wide // heads
    plen = every.shape[1]
    total = plen + rows

    def own(width):
        return pl.BlockSpec((1, rows, width), lambda s, h, b: (s, 0, h))

    small = pl.BlockSpec((1, plen, HD), lambda s, h, b: (s, 0, h))
    spec = pltpu.PrefetchScalarGridSpec(
        num_scalar_prefetch=1,
        grid=(slots, heads),
        in_specs=[
            own(group),
            own(group),
            own(HD),
            own(HD),
            pl.BlockSpec((1, plen, HD), lambda s, h, b: (b[s], 0, h)),
            pl.BlockSpec((1, plen, HD), lambda s, h, b: (b[s], 0, heads + h)),
        ],
        out_specs=[own(group), own(HD), own(HD), small, small],
        scratch_shapes=[
            pltpu.VMEM((total, HD), jnp.bfloat16),
            pltpu.VMEM((HD, total), jnp.bfloat16),
            pltpu.VMEM((total, HD), jnp.bfloat16),
            pltpu.VMEM((total, HD), jnp.float32),
            pltpu.VMEM((total, HD), jnp.float32),
        ],
    )
    shape = jax.ShapeDtypeStruct
    flops = slots * heads * (group // HD) * rows * (plen + rows) * HD * 8
    return pl.pallas_call(
        attention_kernel,
        grid_spec=spec,
        out_shape=[
            shape(queries.shape, jnp.bfloat16),
            shape(resp_keys.shape, jnp.bfloat16),
            shape(resp_keys.shape, jnp.bfloat16),
            shape((slots, plen, heads * HD), jnp.float32),
            shape((slots, plen, heads * HD), jnp.float32),
        ],
        compiler_params=pltpu.CompilerParams(vmem_limit_bytes=48 * 1024 * 1024),
        cost_estimate=pl.CostEstimate(
            flops=flops, bytes_accessed=6 * queries.size, transcendentals=flops // 1024
        ),
    )(blocks, queries, out_grad, resp_keys, resp_values, every, every)


def shards(
    prompt_hidden,
    key_weight,
    value_weight,
    queries,
    resp_keys,
    resp_values,
    out_grad,
    counts,
    slot_of,
    owner,
):
    slots = queries.shape[0]
    prompts = counts.shape[0]
    weight = jnp.concatenate([key_weight, value_weight], axis=1)
    weight_full = lax.all_gather(weight, "seq", axis=0, tiled=True)
    hidden = prompt_hidden[0]
    rows = jnp.dot(hidden, weight_full, preferred_element_type=jnp.float32).astype(jnp.bfloat16)
    first = lax.axis_index("seq") * slots
    blocks = locate(counts, slot_of, owner, first, slots)
    every = lax.all_gather(rows[None], "seq", axis=0, tiled=True)
    grad_query, grad_key, grad_value, prompt_key, prompt_value = attention(
        blocks, queries, out_grad, resp_keys, resp_values, every
    )
    both = jnp.concatenate([prompt_key, prompt_value], axis=2)
    hits = blocks[:, None] == jnp.arange(prompts, dtype=jnp.int32)[None, :]
    terms = jnp.sum(jnp.where(hits[:, :, None, None], both[:, None], 0.0), axis=0)
    moved = lax.all_to_all(terms.astype(jnp.bfloat16), "seq", 0, 0, tiled=True)
    back = jnp.sum(moved.astype(jnp.float32), axis=0).astype(jnp.bfloat16)
    partial_grad = jnp.einsum("lc,dc->ld", back, weight_full, preferred_element_type=jnp.float32)
    prompt_grad = lax.psum_scatter(
        partial_grad[None].astype(jnp.bfloat16), "head", scatter_dimension=2, tiled=True
    )
    return (grad_query, grad_key, grad_value, prompt_grad)


def solution(mesh):
    placed = (
        P(("grp", "seq"), None, None),
        P("seq", "head"),
        P("seq", "head"),
        P(("grp", "seq"), None, "head"),
        P(("grp", "seq"), None, "head"),
        P(("grp", "seq"), None, "head"),
        P(("grp", "seq"), None, "head"),
        P("grp"),
        P("grp"),
        P("grp"),
    )
    return jax.shard_map(
        shards,
        mesh=mesh,
        in_specs=placed,
        out_specs=(P(("grp", "seq"), None, "head"),) * 4,
        check_vma=False,
    )
```

time: 421 us -> 223 us (0.53)
  waiting for transfers between devices: 202 us -> 135 us
  matrix products: 70.9 us -> 10.1 us
  local copies, waits for them, and re-layouts: 45.6 us -> 3.27 us
  blocking collectives: 64.5 us -> 28.7 us
  Pallas kernels: 0 us -> 27.4 us
  other arithmetic: 21.9 us -> 3.55 us
    reduce_scatter x2 -> x0, waiting for transfers between devices: 118 us -> none  [the longest x1 61.8 us: shards(): lax.psum_scatter(term_value, 'seq', scatter_dimension=0, tiled=True)]
    all_gather x2 -> x0, blocking collectives: 64.5 us -> none  [the longest x1 32.8 us: shards(): lax.all_gather(prompt_keys[None], 'seq', axis=0, tiled=True)]
    all_gather x2, waiting for transfers between devices: 78.2 us -> 127 us  [the longest x1 90.4 us: shards(): weight_full = lax.all_gather(weight, 'seq', axis=0, tiled=True)]
    dot_general x16 -> x2, matrix products: 49.8 us -> 10.1 us  [the longest x1 5.41 us: shards(): jnp.einsum('lc,dc->ld', back, weight_full, preferred_element_type=jnp.flo...]
    all_to_all x0 -> x1, blocking collectives: none -> 28.7 us  [shards(): moved = lax.all_to_all(terms.astype(jnp.bfloat16), 'seq', 0, 0, tiled=True)]
    pallas_call x0 -> x1, Pallas kernels: none -> 27.4 us  [attention(): pl.pallas_call(attention_kernel, grid_spec=spec, out_shape=[shape(queries...]
    sub x2 -> x0, matrix products: 21.1 us -> none  [attend(): weights = jnp.exp(scores - highest)]
    convert_element_type x2 -> x0, other arithmetic: 18.7 us -> none  [attend(): probs_b = probs.astype(jnp.bfloat16)]
  transfers between devices with their start and end apart: 5 -> 3, of which waited for: 5 -> 3; matrix products, arithmetic and copies ran while one was open for 4% -> 0% of each run, Pallas kernels for 0% -> 0%
where the time goes in v1:
time: 223 us; the launch traced here: 222 us
  waiting for transfers between devices  135 us (61%)
  blocking collectives  28.7 us (13%)
  Pallas kernels  27.4 us (12%)
  between operations  13.9 us (6%)
  matrix products  10.1 us (5%)
  other arithmetic  3.55 us (2%)
  local copies, waits for them, and re-layouts  3.27 us (1%)
    all_gather x1, waiting for transfers between devices, shards(): weight_full = lax.all_gather(weight, 'seq', axis=0, tiled=True)  90.4 us
    all_gather x1, waiting for transfers between devices, shards(): every = lax.all_gather(rows[None], 'seq', axis=0, tiled=True)  37 us
    all_to_all x1, blocking collectives, shards(): moved = lax.all_to_all(terms.astype(jnp.bfloat16), 'seq', 0, 0, tiled=True)  28.7 us
    pallas_call x1, Pallas kernels, attention(): pl.pallas_call(attention_kernel, grid_spec=spec, out_shape=[shape(queries...  27.4 us
    reduce_scatter x1, waiting for transfers between devices, shards(): lax.psum_scatter(partial_grad[None].astype(jnp.bfloat16), 'head', scatter...  7.86 us
    dot_general x1, matrix products, shards(): jnp.einsum('lc,dc->ld', back, weight_full, preferred_element_type=jnp.flo...  5.41 us
    dot_general x1, matrix products, shards(): jnp.dot(hidden, weight_full, preferred_element_type=jnp.float32)  4.71 us
  transfers between devices with their start and end apart: 3, of which 3 were waited for; matrix products, arithmetic and copies ran while one was open for 0% of the time, Pallas kernels for 0%

profile of v1, /device:TPU:0, one launch (start us, length us, event | category | flops | bytes accessed | tf_op | source)
XLA Modules:
  0.0 222.3 jit_solution(4307499691761614713)
XLA Ops:
  7.2 0.0 copy-start
  7.2 0.0 all-gather.4.cloned.1.call-start
  7.2 2.0 pad_maximum_fusion
  9.3 0.0 all-gather.4.cloned.1.call-update
  9.3 0.0 copy-start.4
  9.3 0.0 copy-start.5
  9.3 0.0 copy-start.6
  9.3 0.0 copy-start.2
  9.3 0.0 copy-start.3
  9.4 0.0 all-gather.6.cloned.1.call-start
  9.4 90.4 %all-gather.4.cloned.1.call-done = bf16[5120,512]{1,0:T(8,128)(2,1)} async-done(((bf16[640,512]{1,0:T(8,128)(2,1)}), bf16[5120,512]{1,0:T(8,128)(2,1)}) %all-gather.4.cloned.1.call-update) | async-done | bytes 5242896 | tf_op jit(solution)/shard_map/all_gather | solution.py:161
  99.8 4.7 %fusion.6 = bf16[128,512]{0,1:T(8,128)(2,1)} fusion(bf16[5120,512]{1,0:T(8,128)(2,1)} %all-gather.4.cloned.1.call-done, bf16[1,128,5120]{2,1,0:T(8,128)(2,1)S(1)} %copy-done), kind=kOutput, calls=%fused_computation.6 | convolution fusion | flops 671154176 | bytes 6684672 | tf_op jit(solution)/shard_map/dot_general | solution.py:163
  104.5 0.0 all-gather.6.cloned.1.call-update
  104.5 0.0 reduce-scatter.2.cloned.1.call-start
  104.6 0.2 reduce-window.8
  104.8 0.2 fusion.9
  104.9 0.2 fusion.10
  105.1 0.0 copy-done.6
  105.1 0.2 fusion.11.blocks_ref
  105.3 0.1 iota_compare_fusion
  105.4 37.0 %all-gather.6.cloned.1.call-done = bf16[1024,512]{0,1:T(8,128)(2,1)} async-done(((bf16[128,512]{0,1:T(8,128)(2,1)}), bf16[1024,512]{0,1:T(8,128)(2,1)}) %all-gather.6.cloned.1.call-update) | async-done | bytes 1048592 | tf_op jit(solution)/shard_map/all_gather | solution.py:166
  142.4 1.5 copy.15
  143.9 0.0 copy-start.1
  143.9 1.7 copy-done.1
  145.6 27.4 %shard_map.129 = (bf16[2,512,1280]{2,1,0:T(8,128)(2,1)}, bf16[2,512,256]{2,1,0:T(8,128)(2,1)}, bf16[2,512,256]{2,1,0:T(8,128)(2,1)}, f32[2,128,256]{2,1,0:T(8,128)S(1)}, f32[2,128,256]{2,1,0:T(8,128)S(1)}) custom-call(s32[2]{0:T(128)S(1)} %fusion.11.blocks_ref, bf16[2,512,1280]{2,1,0:T(8,128)(2,1)S(1)} %copy-done.1, bf16[2,512,1280]{2,1,0:T(8,128)(2,1)} %grad_ref.1, ...), custom_call_target="tpu_custom_call" | custom-call | flops 6710886400 | bytes 7864320 | tf_op jit(solution)/shard_map/pallas_call | solution.py:129
  173.0 0.1 pad_maximum_fusion.1
  173.1 0.5 select_reduce_fusion
  173.6 28.7 %all_to_all.5 = bf16[8,128,512]{2,1,0:T(8,128)(2,1)S(1)} all-to-all(bf16[8,128,512]{2,1,0:T(8,128)(2,1)S(1)} %select_reduce_fusion), channel_id=1, replica_groups=mesh['grp'=2,'seq'=8,'head'=2] {'seq'}, dimensions={0} | all-to-all | bytes 2097152 | tf_op jit(solution)/shard_map/all_to_all | solution.py:173
  202.3 0.1 reduce_sum.52
  202.4 5.4 %fusion = bf16[1,128,5120]{2,1,0:T(8,128)(2,1)} fusion(bf16[128,512]{1,0:T(8,128)(2,1)S(1)} %reduce_sum.52, bf16[5120,512]{1,0:T(8,128)(2,1)} %all-gather.4.cloned.1.call-done), kind=kOutput, calls=%fused_computation.1 | convolution fusion | flops 671744000 | bytes 6684672 | tf_op jit(solution)/shard_map/lc,dc->ld/dot_general | solution.py:175
  207.9 0.0 reduce-scatter.2.cloned.1.call-update
  207.9 7.9 %reduce-scatter.2.cloned.1.call-done = bf16[1,128,2560]{2,1,0:T(8,128)(2,1)} async-done(((bf16[1,128,5120]{2,1,0:T(8,128)(2,1)}), bf16[1,128,2560]{2,1,0:T(8,128)(2,1)}) %reduce-scatter.2.cloned.1.call-update) | async-done | bytes 655376 | tf_op jit(solution)/shard_map/reduce_scatter | solution.py:176
  (6 shorter events, 0.0 us)
Async XLA Ops:
  7.2 92.6 %copy-start = (bf16[1,128,5120]{2,1,0:T(8,128)(2,1)S(1)}, bf16[1,128,5120]{2,1,0:T(8,128)(2,1)}, u32[]{:S(2)}) copy-start(bf16[1,128,5120]{2,1,0:T(8,128)(2,1)} %param.10) | copy-start | bytes 3932164
  7.2 92.6 %all-gather.4.cloned.1.call-start = ((), (), s32[]{:S(2)}) async-start(), calls=%async_computation.2 | async-start | bytes 5898240 | tf_op jit(solution)/shard_map/all_gather | solution.py:161
  9.3 95.3 %copy-start.4 = (s32[8]{0:T(128)S(1)}, s32[8]{0:T(128)}, u32[]{:S(2)}) copy-start(s32[8]{0:T(128)} %param.17) | copy-start | bytes 100
  9.3 95.4 %copy-start.5 = (s32[16]{0:T(128)S(1)}, s32[16]{0:T(128)}, u32[]{:S(2)}) copy-start(s32[16]{0:T(128)} %param.18) | copy-start | bytes 196
  9.3 95.8 %copy-start.6 = (s32[8]{0:T(128)S(1)}, s32[8]{0:T(128)}, u32[]{:S(2)}) copy-start(s32[8]{0:T(128)} %param.19) | copy-start | bytes 100
  9.3 134.5 %copy-start.2 = (bf16[2,512,256]{2,1,0:T(8,128)(2,1)S(1)}, bf16[2,512,256]{2,1,0:T(8,128)(2,1)}, u32[]{:S(2)}) copy-start(bf16[2,512,256]{2,1,0:T(8,128)(2,1)} %key_ref.1) | copy-start | bytes 1572868
  9.3 134.5 %copy-start.3 = (bf16[2,512,256]{2,1,0:T(8,128)(2,1)S(1)}, bf16[2,512,256]{2,1,0:T(8,128)(2,1)}, u32[]{:S(2)}) copy-start(bf16[2,512,256]{2,1,0:T(8,128)(2,1)} %value_ref.1) | copy-start | bytes 1572868
  9.4 133.0 %all-gather.6.cloned.1.call-start = ((), (), s32[]{:S(2)}) async-start(), calls=%async_computation.4 | async-start | bytes 1179648 | tf_op jit(solution)/shard_map/all_gather | solution.py:166
  104.5 111.2 %reduce-scatter.2.cloned.1.call-start = ((), (), s32[]{:S(2)}) async-start(), calls=%async_computation.3 | async-start | bytes 1966080 | tf_op jit(solution)/shard_map/reduce_scatter | solution.py:176
  143.9 1.7 copy-start.1
Sparse Core Ops, SparseCore 0:
  10.8 88.9 all-gather.3
  104.6 37.7 all-gather.5
  208.0 7.6 reduce-scatter.1

commit v2 on v1

--- a/solution.py
+++ b/solution.py
@@ -143,7 +143,210 @@
     )(blocks, queries, out_grad, resp_keys, resp_values, every, every)
 
 
+MESH = pl.DeviceIdType.MESH
+
+
+def project_kernel(
+    count,
+    hidden_ref,
+    key_weight_ref,
+    value_weight_ref,
+    every_ref,
+    key_full,
+    value_full,
+    hidden_all,
+    total,
+    part_out,
+    part_in,
+    own_sem,
+    pair_sem,
+    direct_send,
+    direct_recv,
+    cross_send,
+    cross_recv,
+    line_send,
+    line_recv,
+    side_send,
+    side_recv,
+):
+    plen = hidden_ref.shape[2]
+    rows, width = key_weight_ref.shape
+    half = rows // 2
+    grp = lax.axis_index("grp")
+    seq = lax.axis_index("seq")
+    z, y = lax.div(seq, 2), lax.rem(seq, 2)
+    bit = lax.rem(grp, 2)
+    across = {"grp": grp + 1 - 2 * bit}
+    pair = {"seq": seq + 1 - 2 * y}
+
+    def ahead(k):
+        return {"seq": lax.rem(z + k, count) * 2 + y}
+
+    def behind(k):
+        return lax.rem(z + count - k, count)
+
+    barrier = pltpu.get_barrier_semaphore()
+    for k in range(1, count):
+        pl.semaphore_signal(barrier, inc=1, device_id=ahead(k), device_id_type=MESH)
+    pl.semaphore_signal(barrier, inc=1, device_id=across, device_id_type=MESH)
+    pl.semaphore_signal(barrier, inc=1, device_id=pair, device_id_type=MESH)
+    pl.semaphore_wait(barrier, count + 1)
+
+    def remote(source, target, send, recv, device):
+        return pltpu.make_async_remote_copy(
+            src_ref=source,
+            dst_ref=target,
+            send_sem=send,
+            recv_sem=recv,
+            device_id=device,
+            device_id_type=MESH,
+        )
+
+    mine = pl.ds(pl.multiple_of(bit * half, 16), half)
+    theirs = pl.ds(pl.multiple_of((1 - bit) * half, 16), half)
+    weights = ((key_weight_ref, key_full), (value_weight_ref, value_full))
+    swap = remote(
+        hidden_ref.at[1 - y],
+        hidden_all.at[:, pl.ds(plen, plen), :],
+        pair_sem.at[0],
+        pair_sem.at[1],
+        pair,
+    )
+    direct = {}
+    for k in range(count - 1, 0, -1):
+        for i, (source, target) in enumerate(weights):
+            direct[k, i] = remote(
+                source.at[mine],
+                target.at[z, mine],
+                direct_send.at[i, k],
+                direct_recv.at[i, k],
+                ahead(k),
+            )
+            direct[k, i].start()
+    swap.start()
+    locals_ = [
+        pltpu.make_async_copy(key_weight_ref, key_full.at[z], own_sem.at[0]),
+        pltpu.make_async_copy(value_weight_ref, value_full.at[z], own_sem.at[1]),
+        pltpu.make_async_copy(hidden_ref.at[y], hidden_all.at[:, pl.ds(0, plen), :], own_sem.at[2]),
+    ]
+    for copy in locals_:
+        copy.start()
+    for copy in locals_:
+        copy.wait()
+    swap.wait()
+
+    def add(block, first):
+        rows_in = hidden_all[block]
+        for i, (_, target) in enumerate(weights):
+            lanes = slice(i * width, (i + 1) * width)
+            term = dot(rows_in, target[block], NN)
+            total[:, lanes] = term if first else total[:, lanes] + term
+
+    add(z, True)
+    cross = {}
+    for k in range(1, count):
+        block = behind(k)
+        for i, (source, target) in enumerate(weights):
+            remote(
+                source.at[mine],
+                target.at[block, mine],
+                direct_send.at[i, k],
+                direct_recv.at[i, k],
+                ahead(k),
+            ).wait_recv()
+            cross[k, i] = remote(
+                target.at[block, mine],
+                target.at[block, mine],
+                cross_send.at[i, k],
+                cross_recv.at[i, k],
+                across,
+            )
+            cross[k, i].start()
+    for k in range(1, count):
+        block = behind(k)
+        for i, (_, target) in enumerate(weights):
+            remote(
+                target.at[block, theirs],
+                target.at[block, theirs],
+                cross_send.at[i, k],
+                cross_recv.at[i, k],
+                across,
+            ).wait_recv()
+        add(block, False)
+    part_out[...] = total[plen:, :].astype(jnp.bfloat16)
+    parts = remote(part_out, part_in, pair_sem.at[2], pair_sem.at[3], pair)
+    parts.start()
+    parts.wait()
+    every_ref[seq] = (total[:plen, :] + part_in[...].astype(jnp.float32)).astype(jnp.bfloat16)
+    line, side = {}, {}
+    for k in range(1, count):
+        line[k] = remote(
+            every_ref.at[seq], every_ref.at[seq], line_send.at[k], line_recv.at[k], ahead(k)
+        )
+        line[k].start()
+    for k in range(count):
+        block = behind(k) * 2 + y
+        if k > 0:
+            remote(
+                every_ref.at[block],
+                every_ref.at[block],
+                line_send.at[k],
+                line_recv.at[k],
+                ahead(k),
+            ).wait_recv()
+        side[k] = remote(
+            every_ref.at[block], every_ref.at[block], side_send.at[k], side_recv.at[k], pair
+        )
+        side[k].start()
+    for k in range(count):
+        block = behind(k) * 2 + 1 - y
+        remote(
+            every_ref.at[block], every_ref.at[block], side_send.at[k], side_recv.at[k], pair
+        ).wait_recv()
+    for copy in [*direct.values(), *cross.values(), *line.values(), *side.values()]:
+        copy.wait_send()
+
+
+def project(hidden, key_weight, value_weight, members):
+    count = members // 2
+    plen = hidden.shape[2]
+    rows, width = key_weight.shape
+    shape = jax.ShapeDtypeStruct
+    vmem = pl.BlockSpec(memory_space=pltpu.VMEM)
+    dma = pltpu.SemaphoreType.DMA
+    return pl.pallas_call(
+        functools.partial(project_kernel, count),
+        out_shape=[
+            shape((members, plen, 2 * width), jnp.bfloat16),
+            shape((count, rows, width), jnp.bfloat16),
+            shape((count, rows, width), jnp.bfloat16),
+        ],
+        in_specs=[vmem] * 3,
+        out_specs=[vmem] * 3,
+        scratch_shapes=[
+            pltpu.VMEM((count, 2 * plen, rows), jnp.bfloat16),
+            pltpu.VMEM((2 * plen, 2 * width), jnp.float32),
+            pltpu.VMEM((plen, 2 * width), jnp.bfloat16),
+            pltpu.VMEM((plen, 2 * width), jnp.bfloat16),
+            dma((3,)),
+            dma((4,)),
+            dma((2, count)),
+            dma((2, count)),
+            dma((2, count)),
+            dma((2, count)),
+            dma((count,)),
+            dma((count,)),
+            dma((count,)),
+            dma((count,)),
+        ],
+        compiler_params=pltpu.CompilerParams(
+            collective_id=0, has_side_effects=True, vmem_limit_bytes=48 * 1024 * 1024
+        ),
+    )(hidden, key_weight, value_weight)
+
+
 def shards(
+    members,
     prompt_hidden,
     key_weight,
     value_weight,
@@ -157,13 +360,13 @@
 ):
     slots = queries.shape[0]
     prompts = counts.shape[0]
-    weight = jnp.concatenate([key_weight, value_weight], axis=1)
-    weight_full = lax.all_gather(weight, "seq", axis=0, tiled=True)
-    hidden = prompt_hidden[0]
-    rows = jnp.dot(hidden, weight_full, preferred_element_type=jnp.float32).astype(jnp.bfloat16)
-    first = lax.axis_index("seq") * slots
-    blocks = locate(counts, slot_of, owner, first, slots)
-    every = lax.all_gather(rows[None], "seq", axis=0, tiled=True)
+    plen, model = prompt_hidden.shape[1:]
+    rows, width = key_weight.shape
+    count = members // 2
+    hidden = prompt_hidden[0].reshape(plen, count, 2, rows).transpose(2, 1, 0, 3)
+    every, key_half, value_half = project(hidden, key_weight, value_weight, members)
+    seq = lax.axis_index("seq")
+    blocks = locate(counts, slot_of, owner, seq * slots, slots)
     grad_query, grad_key, grad_value, prompt_key, prompt_value = attention(
         blocks, queries, out_grad, resp_keys, resp_values, every
     )
@@ -172,10 +375,19 @@
     terms = jnp.sum(jnp.where(hits[:, :, None, None], both[:, None], 0.0), axis=0)
     moved = lax.all_to_all(terms.astype(jnp.bfloat16), "seq", 0, 0, tiled=True)
     back = jnp.sum(moved.astype(jnp.float32), axis=0).astype(jnp.bfloat16)
-    partial_grad = jnp.einsum("lc,dc->ld", back, weight_full, preferred_element_type=jnp.float32)
-    prompt_grad = lax.psum_scatter(
-        partial_grad[None].astype(jnp.bfloat16), "head", scatter_dimension=2, tiled=True
-    )
+    pairs = [(i, i ^ 1) for i in range(members)]
+    back = jnp.concatenate([back, lax.ppermute(back, "seq", pairs)], axis=0)
+    partial_grad = jnp.einsum(
+        "lc,zdc->zld", back[:, :width], key_half, preferred_element_type=jnp.float32
+    ) + jnp.einsum("lc,zdc->zld", back[:, width:], value_half, preferred_element_type=jnp.float32)
+    summed = lax.psum_scatter(
+        partial_grad.astype(jnp.bfloat16), "head", scatter_dimension=0, tiled=True
+    )
+    own = summed[:, :plen]
+    other = lax.ppermute(summed[:, plen:], "seq", pairs)
+    even = lax.rem(seq, 2) == 0
+    placed = jnp.stack([jnp.where(even, own, other), jnp.where(even, other, own)])
+    prompt_grad = placed.transpose(2, 1, 0, 3).reshape(1, plen, model // 2)
     return (grad_query, grad_key, grad_value, prompt_grad)
 
 
@@ -193,7 +405,7 @@
         P("grp"),
     )
     return jax.shard_map(
-        shards,
+        functools.partial(shards, mesh.shape["seq"]),
         mesh=mesh,
         in_specs=placed,
         out_specs=(P(("grp", "seq"), None, "head"),) * 4,

time: 223 us -> 184 us (0.83)
  waiting for transfers between devices: 135 us -> 18.7 us
  Pallas kernels: 27.4 us -> 96.8 us
  matrix products: 10.1 us -> 2.12 us
  blocking collectives: 28.7 us -> 35 us
  local copies, waits for them, and re-layouts: 3.27 us -> 8.51 us
  starting transfers between devices: 0.12 us -> 3.33 us
    all_gather x2 -> x0, waiting for transfers between devices: 127 us -> none  [the longest x1 90.4 us: shards(): weight_full = lax.all_gather(weight, 'seq', axis=0, tiled=True)]
    pallas_call x0 -> x1, Pallas kernels: none -> 69.4 us  [project(): pl.pallas_call(functools.partial(project_kernel, count), out_shape=[shape...]
    ppermute x0 -> x2, waiting for transfers between devices: none -> 11.7 us  [the longest x1 8.16 us: shards(): other = lax.ppermute(summed[:, plen:], 'seq', pairs)]
    dot_general x2, matrix products: 10.1 us -> 2.12 us  [the longest x1 1.6 us: shards(): jnp.einsum('lc,zdc->zld', back[:, :width], key_half, preferred_element_ty...]
    all_to_all x1, blocking collectives: 28.7 us -> 35 us  [shards(): moved = lax.all_to_all(terms.astype(jnp.bfloat16), 'seq', 0, 0, tiled=True)]
    unnamed x14 -> x16, local copies, waits for them, and re-layouts: 1.78 us -> 6.73 us
    ppermute x0 -> x2, starting transfers between devices: none -> 3.29 us  [the longest x1 1.81 us: shards(): other = lax.ppermute(summed[:, plen:], 'seq', pairs)]
where the time goes in v2:
time: 184 us; the launch traced here: 183 us
  Pallas kernels  96.8 us (53%)
  blocking collectives  35 us (19%)
  waiting for transfers between devices  18.7 us (10%)
  between operations  14.2 us (8%)
  local copies, waits for them, and re-layouts  8.51 us (5%)
  other arithmetic  4.55 us (2%)
  starting transfers between devices  3.33 us (2%)
  matrix products  2.12 us (1%)
    pallas_call x1, Pallas kernels, project(): pl.pallas_call(functools.partial(project_kernel, count), out_shape=[shape...  69.4 us
    all_to_all x1, blocking collectives, shards(): moved = lax.all_to_all(terms.astype(jnp.bfloat16), 'seq', 0, 0, tiled=True)  35 us
    pallas_call x1, Pallas kernels, attention(): pl.pallas_call(attention_kernel, grid_spec=spec, out_shape=[shape(queries...  27.4 us
    ppermute x1, waiting for transfers between devices, shards(): other = lax.ppermute(summed[:, plen:], 'seq', pairs)  8.16 us
    reduce_scatter x1, waiting for transfers between devices, shards(): lax.psum_scatter(partial_grad.astype(jnp.bfloat16), 'head', scatter_dimen...  6.96 us
    unnamed x16, local copies, waits for them, and re-layouts  6.73 us
  transfers between devices with their start and end apart: 3, of which 3 were waited for; matrix products, arithmetic and copies ran while one was open for 0% of the time, Pallas kernels for 0%

profile of v2, /device:TPU:0, one launch (start us, length us, event | category | flops | bytes accessed | tf_op | source)
XLA Modules:
  0.0 183.2 jit_solution(1289717320690634715)
XLA Ops:
  7.2 0.0 reduce-scatter.2.cloned.1.call-start
  7.2 0.8 fusion.8
  8.1 0.8 reduce-window.8
  8.9 0.2 fusion.9
  9.1 0.8 fusion.10.blocks_ref
  9.9 0.1 iota_compare_fusion
  10.0 1.8 copy.18
  11.8 0.7 copy.19
  12.5 0.0 copy-start.5
  12.6 0.2 copy-done.2
  12.7 0.1 copy-done.3
  12.8 69.4 %shard_map.129 = (bf16[8,128,512]{2,1,0:T(8,128)(2,1)S(1)}, bf16[4,640,256]{2,1,0:T(8,128)(2,1)S(1)}, bf16[4,640,256]{2,1,0:T(8,128)(2,1)S(1)}) custom-call(bf16[2,4,128,640]{3,2,1,0:T(8,128)(2,1)S(1)} %bitcast.21, bf16[640,256]{1,0:T(8,128)(2,1)S(1)} %copy-done.2, bf16[640,256]{1,0:T(8,128)(2,1)S(1)} %copy-done.3), custom_call_target="tpu_custom_call" | custom-call | tf_op jit(solution)/shard_map/pallas_call | solution.py:317
  82.3 1.1 copy-done
  83.3 1.7 copy-done.4
  85.1 27.4 %shard_map.130 = (bf16[2,512,1280]{2,1,0:T(8,128)(2,1)}, bf16[2,512,256]{2,1,0:T(8,128)(2,1)}, bf16[2,512,256]{2,1,0:T(8,128)(2,1)}, f32[2,128,256]{2,1,0:T(8,128)S(1)}, f32[2,128,256]{2,1,0:T(8,128)S(1)}) custom-call(s32[2]{0:T(128)S(1)} %fusion.10.blocks_ref, bf16[2,512,1280]{2,1,0:T(8,128)(2,1)S(1)} %copy-done.4, bf16[2,512,1280]{2,1,0:T(8,128)(2,1)} %grad_ref.1, ...), custom_call_target="tpu_custom_call" | custom-call | flops 6710886400 | bytes 7864320 | tf_op jit(solution)/shard_map/pallas_call | solution.py:129
  112.5 0.1 pad_maximum_fusion
  112.5 0.5 select_reduce_fusion
  113.0 35.0 %all_to_all.5 = bf16[8,128,512]{2,1,0:T(8,128)(2,1)S(1)} all-to-all(bf16[8,128,512]{2,1,0:T(8,128)(2,1)S(1)} %select_reduce_fusion), channel_id=1, replica_groups=mesh['grp'=2,'seq'=8,'head'=2] {'seq'}, dimensions={0} | all-to-all | bytes 2097152 | tf_op jit(solution)/shard_map/all_to_all | solution.py:376
  148.1 0.1 reduce_sum.52
  148.2 1.5 collective-permute-start
  149.7 3.6 %collective-permute-done = bf16[128,512]{1,0:T(8,128)(2,1)S(1)} collective-permute-done((bf16[128,512]{1,0:T(8,128)(2,1)S(1)}, bf16[128,512]{1,0:T(8,128)(2,1)S(1)}, u32[]{:S(2)}, u32[]{:S(2)}) %collective-permute-start) | collective-permute-done | bytes 131104 | tf_op jit(solution)/shard_map/ppermute | solution.py:379
  153.2 0.5 fusion.5
  153.8 0.8 copy-done.1
  154.6 1.6 fusion
  156.2 0.0 reduce-scatter.2.cloned.1.call-update
  156.2 7.0 %reduce-scatter.2.cloned.1.call-done = bf16[2,256,640]{1,2,0:T(8,128)(2,1)} async-done(((bf16[4,256,640]{1,2,0:T(8,128)(2,1)}), bf16[2,256,640]{1,2,0:T(8,128)(2,1)}) %reduce-scatter.2.cloned.1.call-update) | async-done | bytes 655376 | tf_op jit(solution)/shard_map/reduce_scatter | solution.py:383
  163.1 1.0 slice.19
  164.1 1.8 collective-permute-start.1
  165.9 8.2 %collective-permute-done.1 = bf16[2,128,640]{1,2,0:T(8,128)(2,1)S(1)} collective-permute-done((bf16[2,128,640]{1,2,0:T(8,128)(2,1)S(1)}, bf16[2,128,640]{1,2,0:T(8,128)(2,1)S(1)}, u32[]{:S(2)}, u32[]{:S(2)}) %collective-permute-start.1) | collective-permute-done | bytes 327712 | tf_op jit(solution)/shard_map/ppermute | solution.py:387
  174.1 1.0 select_bitcast_fusion.1
  175.1 0.1 maximum_bitcast_fusion
  175.3 1.1 copy.21
  (10 shorter events, 0.1 us)
Async XLA Ops:
  7.2 156.0 %reduce-scatter.2.cloned.1.call-start = ((), (), s32[]{:S(2)}) async-start(), calls=%async_computation.2 | async-start | bytes 1966080 | tf_op jit(solution)/shard_map/reduce_scatter | solution.py:383
  11.8 1.0 copy-start.2
  11.8 1.1 copy-start.3
  12.5 70.8 %copy-start.5 = (bf16[2,512,256]{2,1,0:T(8,128)(2,1)S(1)}, bf16[2,512,256]{2,1,0:T(8,128)(2,1)}, u32[]{:S(2)}) copy-start(bf16[2,512,256]{2,1,0:T(8,128)(2,1)} %key_ref.1) | copy-start | bytes 1572868
  12.6 70.8 %copy-start.6 = (bf16[2,512,256]{2,1,0:T(8,128)(2,1)S(1)}, bf16[2,512,256]{2,1,0:T(8,128)(2,1)}, u32[]{:S(2)}) copy-start(bf16[2,512,256]{2,1,0:T(8,128)(2,1)} %value_ref.1) | copy-start | bytes 1572868
  82.3 1.1 copy-start
  83.3 1.7 copy-start.4
  148.2 5.0 %collective-permute-start = (bf16[128,512]{1,0:T(8,128)(2,1)S(1)}, bf16[128,512]{1,0:T(8,128)(2,1)S(1)}, u32[]{:S(2)}, u32[]{:S(2)}) collective-permute-start(bf16[128,512]{1,0:T(8,128)(2,1)S(1)} %reduce_sum.52), channel_id=1, source_target_pairs={{0,2},{2,0},{4,6},{6,4},{8,10},{10,8},{12,14},{14,12},{1,3},{3,1},... | collective-permute-start | bytes 393224 | tf_op jit(solution)/shard_map/ppermute | solution.py:379
  153.2 1.3 copy-start.1
  164.1 10.0 %collective-permute-start.1 = (bf16[2,128,640]{1,2,0:T(8,128)(2,1)S(1)}, bf16[2,128,640]{1,2,0:T(8,128)(2,1)S(1)}, u32[]{:S(2)}, u32[]{:S(2)}) collective-permute-start(bf16[2,128,640]{1,2,0:T(8,128)(2,1)S(1)} %slice.19), channel_id=1, source_target_pairs={{0,2},{2,0},{4,6},{6,4},{8,10},{10,8},{12,14},{14,12},{1,3},{3,1},... | collective-permute-start | bytes 983048 | tf_op jit(solution)/shard_map/ppermute | solution.py:387
Sparse Core Ops, SparseCore 0:
  156.3 6.7 reduce-scatter.1

commit v3 on v2

--- a/solution.py
+++ b/solution.py
@@ -179,15 +179,20 @@
     across = {"grp": grp + 1 - 2 * bit}
     pair = {"seq": seq + 1 - 2 * y}
 
-    def ahead(k):
-        return {"seq": lax.rem(z + k, count) * 2 + y}
-
-    def behind(k):
-        return lax.rem(z + count - k, count)
+    up = {"seq": lax.rem(z + 1, count) * 2 + y}
+    down = {"seq": lax.rem(z + count - 1, count) * 2 + y}
+    has_up, has_down = z < count - 1, z > 0
+
+    def arrivals(k):
+        return (
+            (z >= k, lax.rem(z + count - k, count), has_up, up, 0),
+            (z + k < count, lax.rem(z + k, count), has_down, down, 1),
+        )
 
     barrier = pltpu.get_barrier_semaphore()
     for k in range(1, count):
-        pl.semaphore_signal(barrier, inc=1, device_id=ahead(k), device_id_type=MESH)
+        other = {"seq": lax.rem(z + k, count) * 2 + y}
+        pl.semaphore_signal(barrier, inc=1, device_id=other, device_id_type=MESH)
     pl.semaphore_signal(barrier, inc=1, device_id=across, device_id_type=MESH)
     pl.semaphore_signal(barrier, inc=1, device_id=pair, device_id_type=MESH)
     pl.semaphore_wait(barrier, count + 1)
@@ -212,17 +217,22 @@
         pair_sem.at[1],
         pair,
     )
-    direct = {}
-    for k in range(count - 1, 0, -1):
-        for i, (source, target) in enumerate(weights):
-            direct[k, i] = remote(
+    sent = []
+
+    def start(copy, wanted):
+        pl.when(wanted)(copy.start)
+        sent.append((copy, wanted))
+
+    for i, (source, target) in enumerate(weights):
+        for wanted, device, way in ((has_up, up, 0), (has_down, down, 1)):
+            copy = remote(
                 source.at[mine],
                 target.at[z, mine],
-                direct_send.at[i, k],
-                direct_recv.at[i, k],
-                ahead(k),
+                direct_send.at[i, way, 0],
+                direct_recv.at[i, z],
+                device,
             )
-            direct[k, i].start()
+            start(copy, wanted)
     swap.start()
     locals_ = [
         pltpu.make_async_copy(key_weight_ref, key_full.at[z], own_sem.at[0]),
@@ -242,69 +252,56 @@
             term = dot(rows_in, target[block], NN)
             total[:, lanes] = term if first else total[:, lanes] + term
 
+    def settle(k):
+        for there, block, _, _, _ in arrivals(k):
+
+            @pl.when(there)
+            def _():
+                for i, (_, target) in enumerate(weights):
+                    view = target.at[block, theirs]
+                    remote(
+                        view, view, cross_send.at[i, block], cross_recv.at[i, block], across
+                    ).wait_recv()
+                add(block, False)
+
     add(z, True)
-    cross = {}
     for k in range(1, count):
-        block = behind(k)
-        for i, (source, target) in enumerate(weights):
-            remote(
-                source.at[mine],
-                target.at[block, mine],
-                direct_send.at[i, k],
-                direct_recv.at[i, k],
-                ahead(k),
-            ).wait_recv()
-            cross[k, i] = remote(
-                target.at[block, mine],
-                target.at[block, mine],
-                cross_send.at[i, k],
-                cross_recv.at[i, k],
-                across,
-            )
-            cross[k, i].start()
-    for k in range(1, count):
-        block = behind(k)
         for i, (_, target) in enumerate(weights):
-            remote(
-                target.at[block, theirs],
-                target.at[block, theirs],
-                cross_send.at[i, k],
-                cross_recv.at[i, k],
-                across,
-            ).wait_recv()
-        add(block, False)
+            for there, block, further, device, way in arrivals(k):
+                view = target.at[block, mine]
+                onward = remote(
+                    view, view, direct_send.at[i, way, k], direct_recv.at[i, block], device
+                )
+                pl.when(there)(onward.wait_recv)
+                start(onward, jnp.logical_and(there, further))
+                copy = remote(
+                    view, view, cross_send.at[i, block], cross_recv.at[i, block], across
+                )
+                start(copy, there)
+        if k > 1:
+            settle(k - 1)
+    settle(count - 1)
     part_out[...] = total[plen:, :].astype(jnp.bfloat16)
     parts = remote(part_out, part_in, pair_sem.at[2], pair_sem.at[3], pair)
     parts.start()
     parts.wait()
     every_ref[seq] = (total[:plen, :] + part_in[...].astype(jnp.float32)).astype(jnp.bfloat16)
-    line, side = {}, {}
+    view = every_ref.at[seq]
+    for wanted, device, way in ((has_up, up, 0), (has_down, down, 1)):
+        start(remote(view, view, line_send.at[way, 0], line_recv.at[z], device), wanted)
+    start(remote(view, view, side_send.at[z], side_recv.at[z], pair), z >= 0)
     for k in range(1, count):
-        line[k] = remote(
-            every_ref.at[seq], every_ref.at[seq], line_send.at[k], line_recv.at[k], ahead(k)
-        )
-        line[k].start()
-    for k in range(count):
-        block = behind(k) * 2 + y
-        if k > 0:
-            remote(
-                every_ref.at[block],
-                every_ref.at[block],
-                line_send.at[k],
-                line_recv.at[k],
-                ahead(k),
-            ).wait_recv()
-        side[k] = remote(
-            every_ref.at[block], every_ref.at[block], side_send.at[k], side_recv.at[k], pair
-        )
-        side[k].start()
-    for k in range(count):
-        block = behind(k) * 2 + 1 - y
-        remote(
-            every_ref.at[block], every_ref.at[block], side_send.at[k], side_recv.at[k], pair
-        ).wait_recv()
-    for copy in [*direct.values(), *cross.values(), *line.values(), *side.values()]:
-        copy.wait_send()
+        for there, block, further, device, way in arrivals(k):
+            view = every_ref.at[block * 2 + y]
+            onward = remote(view, view, line_send.at[way, k], line_recv.at[block], device)
+            pl.when(there)(onward.wait_recv)
+            start(onward, jnp.logical_and(there, further))
+            start(remote(view, view, side_send.at[block], side_recv.at[block], pair), there)
+    for block in range(count):
+        view = every_ref.at[block * 2 + 1 - y]
+        remote(view, view, side_send.at[block], side_recv.at[block], pair).wait_recv()
+    for copy, wanted in sent:
+        pl.when(wanted)(copy.wait_send)
 
 
 def project(hidden, key_weight, value_weight, members):
@@ -330,11 +327,11 @@
             pltpu.VMEM((plen, 2 * width), jnp.bfloat16),
             dma((3,)),
             dma((4,)),
+            dma((2, 2, count)),
             dma((2, count)),
             dma((2, count)),
             dma((2, count)),
             dma((2, count)),
-            dma((count,)),
             dma((count,)),
             dma((count,)),
             dma((count,)),

time: 184 us -> 170 us (0.924)
  blocking collectives: 35 us -> 25 us
  Pallas kernels: 96.8 us -> 93.5 us
    all_to_all x1, blocking collectives: 35 us -> 25 us  [shards(): moved = lax.all_to_all(terms.astype(jnp.bfloat16), 'seq', 0, 0, tiled=True)]
    pallas_call x1, Pallas kernels: 69.4 us -> 66.1 us  [project(): pl.pallas_call(functools.partial(project_kernel, count), out_shape=[shape...]
where the time goes in v3:
time: 170 us
  Pallas kernels  93.5 us (55%)
  blocking collectives  25 us (15%)
  waiting for transfers between devices  18.7 us (11%)
  between operations  14.2 us (8%)
  local copies, waits for them, and re-layouts  8.51 us (5%)
  other arithmetic  4.55 us (3%)
  starting transfers between devices  3.37 us (2%)
  matrix products  2.12 us (1%)
    pallas_call x1, Pallas kernels, project(): pl.pallas_call(functools.partial(project_kernel, count), out_shape=[shape...  66.1 us
    pallas_call x1, Pallas kernels, attention(): pl.pallas_call(attention_kernel, grid_spec=spec, out_shape=[shape(queries...  27.4 us
    all_to_all x1, blocking collectives, shards(): moved = lax.all_to_all(terms.astype(jnp.bfloat16), 'seq', 0, 0, tiled=True)  25 us
    ppermute x1, waiting for transfers between devices, shards(): other = lax.ppermute(summed[:, plen:], 'seq', pairs)  8.17 us
    reduce_scatter x1, waiting for transfers between devices, shards(): lax.psum_scatter(partial_grad.astype(jnp.bfloat16), 'head', scatter_dimen...  7.02 us
    unnamed x16, local copies, waits for them, and re-layouts  6.73 us
    ppermute x1, waiting for transfers between devices, shards(): back = jnp.concatenate([back, lax.ppermute(back, 'seq', pairs)], axis=0)  3.51 us
  transfers between devices with their start and end apart: 3, of which 3 were waited for; matrix products, arithmetic and copies ran while one was open for 0% of the time, Pallas kernels for 0%

profile of v3, /device:TPU:0, one launch (start us, length us, event | category | flops | bytes accessed | tf_op | source)
XLA Modules:
  0.0 169.9 jit_solution(4195811204291903782)
XLA Ops:
  7.2 0.0 reduce-scatter.2.cloned.1.call-start
  7.2 0.8 fusion.8
  8.1 0.8 reduce-window.8
  8.9 0.2 fusion.9
  9.1 0.8 fusion.10.blocks_ref
  9.9 0.1 iota_compare_fusion
  10.0 1.8 %copy.18 = bf16[1,128,5120]{1,2,0:T(8,128)(2,1)S(1)} copy(bf16[1,128,5120]{2,1,0:T(8,128)(2,1)} %param.10) | data formatting | bytes 2621440 | tf_op args[0]
  11.8 0.0 copy-start.2
  11.8 0.7 copy.19
  12.6 0.2 copy-done.2
  12.7 0.1 copy-done.3
  12.8 66.1 %shard_map.129 = (bf16[8,128,512]{2,1,0:T(8,128)(2,1)S(1)}, bf16[4,640,256]{2,1,0:T(8,128)(2,1)S(1)}, bf16[4,640,256]{2,1,0:T(8,128)(2,1)S(1)}) custom-call(bf16[2,4,128,640]{3,2,1,0:T(8,128)(2,1)S(1)} %bitcast.21, bf16[640,256]{1,0:T(8,128)(2,1)S(1)} %copy-done.2, bf16[640,256]{1,0:T(8,128)(2,1)S(1)} %copy-done.3), custom_call_target="tpu_custom_call" | custom-call | tf_op jit(solution)/shard_map/pallas_call | solution.py:314
  79.0 1.1 copy-done
  80.0 1.7 %copy-done.4 = bf16[2,512,1280]{2,1,0:T(8,128)(2,1)S(1)} copy-done((bf16[2,512,1280]{2,1,0:T(8,128)(2,1)S(1)}, bf16[2,512,1280]{2,1,0:T(8,128)(2,1)}, u32[]{:S(2)}) %copy-start.4) | copy-done | bytes 2621464
  81.8 27.4 %shard_map.130 = (bf16[2,512,1280]{2,1,0:T(8,128)(2,1)}, bf16[2,512,256]{2,1,0:T(8,128)(2,1)}, bf16[2,512,256]{2,1,0:T(8,128)(2,1)}, f32[2,128,256]{2,1,0:T(8,128)S(1)}, f32[2,128,256]{2,1,0:T(8,128)S(1)}) custom-call(s32[2]{0:T(128)S(1)} %fusion.10.blocks_ref, bf16[2,512,1280]{2,1,0:T(8,128)(2,1)S(1)} %copy-done.4, bf16[2,512,1280]{2,1,0:T(8,128)(2,1)} %grad_ref.1, ...), custom_call_target="tpu_custom_call" | custom-call | flops 6710886400 | bytes 7864320 | tf_op jit(solution)/shard_map/pallas_call | solution.py:129
  109.2 0.1 pad_maximum_fusion
  109.2 0.5 select_reduce_fusion
  109.7 25.0 %all_to_all.5 = bf16[8,128,512]{2,1,0:T(8,128)(2,1)S(1)} all-to-all(bf16[8,128,512]{2,1,0:T(8,128)(2,1)S(1)} %select_reduce_fusion), channel_id=1, replica_groups=mesh['grp'=2,'seq'=8,'head'=2] {'seq'}, dimensions={0} | all-to-all | bytes 2097152 | tf_op jit(solution)/shard_map/all_to_all | solution.py:373
  134.7 0.1 reduce_sum.52
  134.8 1.5 collective-permute-start
  136.4 3.5 %collective-permute-done = bf16[128,512]{1,0:T(8,128)(2,1)S(1)} collective-permute-done((bf16[128,512]{1,0:T(8,128)(2,1)S(1)}, bf16[128,512]{1,0:T(8,128)(2,1)S(1)}, u32[]{:S(2)}, u32[]{:S(2)}) %collective-permute-start) | collective-permute-done | bytes 131104 | tf_op jit(solution)/shard_map/ppermute | solution.py:376
  139.9 0.5 fusion.5
  140.4 0.8 copy-done.1
  141.2 1.6 fusion
  142.8 0.0 reduce-scatter.2.cloned.1.call-update
  142.8 7.0 %reduce-scatter.2.cloned.1.call-done = bf16[2,256,640]{1,2,0:T(8,128)(2,1)} async-done(((bf16[4,256,640]{1,2,0:T(8,128)(2,1)}), bf16[2,256,640]{1,2,0:T(8,128)(2,1)}) %reduce-scatter.2.cloned.1.call-update) | async-done | bytes 655376 | tf_op jit(solution)/shard_map/reduce_scatter | solution.py:380
  149.8 1.0 slice.19
  150.8 1.8 %collective-permute-start.1 = (bf16[2,128,640]{1,2,0:T(8,128)(2,1)S(1)}, bf16[2,128,640]{1,2,0:T(8,128)(2,1)S(1)}, u32[]{:S(2)}, u32[]{:S(2)}) collective-permute-start(bf16[2,128,640]{1,2,0:T(8,128)(2,1)S(1)} %slice.19), channel_id=1, source_target_pairs={{0,2},{2,0},{4,6},{6,4},{8,10},{10,8},{12,14},{14,12},{1,3},{3,1},... | collective-permute-start | bytes 983048 | tf_op jit(solution)/shard_map/ppermute | solution.py:384
  152.6 8.2 %collective-permute-done.1 = bf16[2,128,640]{1,2,0:T(8,128)(2,1)S(1)} collective-permute-done((bf16[2,128,640]{1,2,0:T(8,128)(2,1)S(1)}, bf16[2,128,640]{1,2,0:T(8,128)(2,1)S(1)}, u32[]{:S(2)}, u32[]{:S(2)}) %collective-permute-start.1) | collective-permute-done | bytes 327712 | tf_op jit(solution)/shard_map/ppermute | solution.py:384
  160.8 1.0 select_bitcast_fusion.1
  161.8 0.1 maximum_bitcast_fusion
  162.0 1.1 copy.21
  (10 shorter events, 0.1 us)
Async XLA Ops:
  7.2 142.7 %reduce-scatter.2.cloned.1.call-start = ((), (), s32[]{:S(2)}) async-start(), calls=%async_computation.2 | async-start | bytes 1966080 | tf_op jit(solution)/shard_map/reduce_scatter | solution.py:380
  11.8 1.0 copy-start.2
  11.8 1.1 copy-start.3
  12.5 67.5 %copy-start.5 = (bf16[2,512,256]{2,1,0:T(8,128)(2,1)S(1)}, bf16[2,512,256]{2,1,0:T(8,128)(2,1)}, u32[]{:S(2)}) copy-start(bf16[2,512,256]{2,1,0:T(8,128)(2,1)} %key_ref.1) | copy-start | bytes 1572868
  12.6 67.5 %copy-start.6 = (bf16[2,512,256]{2,1,0:T(8,128)(2,1)S(1)}, bf16[2,512,256]{2,1,0:T(8,128)(2,1)}, u32[]{:S(2)}) copy-start(bf16[2,512,256]{2,1,0:T(8,128)(2,1)} %value_ref.1) | copy-start | bytes 1572868
  78.9 1.1 copy-start
  80.0 1.7 %copy-start.4 = (bf16[2,512,1280]{2,1,0:T(8,128)(2,1)S(1)}, bf16[2,512,1280]{2,1,0:T(8,128)(2,1)}, u32[]{:S(2)}) copy-start(bf16[2,512,1280]{2,1,0:T(8,128)(2,1)} %query_ref.1) | copy-start | bytes 7864324
  134.8 5.0 %collective-permute-start = (bf16[128,512]{1,0:T(8,128)(2,1)S(1)}, bf16[128,512]{1,0:T(8,128)(2,1)S(1)}, u32[]{:S(2)}, u32[]{:S(2)}) collective-permute-start(bf16[128,512]{1,0:T(8,128)(2,1)S(1)} %reduce_sum.52), channel_id=1, source_target_pairs={{0,2},{2,0},{4,6},{6,4},{8,10},{10,8},{12,14},{14,12},{1,3},{3,1},... | collective-permute-start | bytes 393224 | tf_op jit(solution)/shard_map/ppermute | solution.py:376
  139.9 1.3 copy-start.1
  150.8 10.0 %collective-permute-start.1 = (bf16[2,128,640]{1,2,0:T(8,128)(2,1)S(1)}, bf16[2,128,640]{1,2,0:T(8,128)(2,1)S(1)}, u32[]{:S(2)}, u32[]{:S(2)}) collective-permute-start(bf16[2,128,640]{1,2,0:T(8,128)(2,1)S(1)} %slice.19), channel_id=1, source_target_pairs={{0,2},{2,0},{4,6},{6,4},{8,10},{10,8},{12,14},{14,12},{1,3},{3,1},... | collective-permute-start | bytes 983048 | tf_op jit(solution)/shard_map/ppermute | solution.py:384
Sparse Core Ops, SparseCore 0:
  142.9 6.8 reduce-scatter.1
